TPU v7x, 32 devices: a whole 2x2x4 slice. The times are simulated.
32 devices in a mesh: gx: 4 (over z), gy: 2 (over y), gz: 4 (over x, core).
Axes of the slice: x: 2, y: 2, z: 4, core: 2. Of those that a mesh axis runs over, the one named last changes fastest.
Arguments:
- e_field: float32 [3, 32, 128, 256], P(None, 'gx', 'gz', 'gy'), may hold values from -6 to 6
- h_field: float32 [3, 32, 128, 256], P(None, 'gx', 'gz', 'gy'), may hold values from -6 to 6
- e_forward: float32 [3, 32, 128, 256], P(None, 'gx', 'gz', 'gy'), may hold values from -6 to 6
- e_coeff: float32 [32, 128, 256], P('gx', 'gz', 'gy'), may hold values from 0.1 to 0.5
- h_coeff: float32 [32, 128, 256], P('gx', 'gz', 'gy'), may hold values from 0.1 to 0.5
- dft_acc: float32 [16, 32, 128, 256], P(None, 'gx', 'gz', 'gy'), may hold values from -6 to 6
- design_mask: int32 [4, 4, 32], P('gx', 'gz', 'gy'), may hold values 0 or 1
- omega_t: float32 [8], replicated, may hold values from -3.140625 to 3.140625
- port_index: int32 [4], replicated, may hold values from 0 to 31
- port_owner: int32 [4], replicated, may hold values from 0 to 31
- port_modes: float32 [4, 2, 128, 256], P(None, None, 'gz', 'gy'), may hold values from -0.0234375 to 0.0234375
- monitor_acc: float32 [32, 16], P(('gx', 'gy', 'gz')), may hold values from -6 to 6
Outputs:
- e_next: float32 [3, 32, 128, 256], P(None, 'gx', 'gz', 'gy')
- h_next: float32 [3, 32, 128, 256], P(None, 'gx', 'gz', 'gy')
- dft_next: float32 [16, 32, 128, 256], P(None, 'gx', 'gz', 'gy')
- monitor_next: float32 [32, 16], P(('gx', 'gy', 'gz'))
All inputs are finite; a program needn't handle non-finite values. No bound on the sum of `design_mask` on one device may be relied on, other than what follows from the above.
Results may differ from a plain program's by a relative error of at most 0.00011.
Values sent between devices are 32-bit elements; how exact they have to be, the bound alone decides.
A program may use at most 64 MiB of HBM per device.

v0:
```python
import functools

import jax
import jax.numpy as jnp
from jax import lax
from jax.experimental import pallas as pl
from jax.experimental.pallas import tpu as pltpu
from jax.sharding import PartitionSpec as P

BY = 8
NF = 8
NP = 4
UNROLL = 32


def tiles(plane):
    return [plane[8 * q : 8 * q + 8] for q in range(plane.shape[0] // 8)]


def pack_lane(fields, lane_of, lane):
    packed = jnp.zeros((8, 128), jnp.float32)
    k = 0
    for plane in fields:
        for tile in tiles(plane):
            moved = pltpu.roll(tile, (k - lane_of) % 128, 1)
            packed = jnp.where(lane == k, moved, packed)
            k += 1
    return packed


def unpack_lane(packed, first, count, lane_of, keep):
    out = [pltpu.roll(packed, (lane_of - first - q) % 128, 1) for q in range(count)]
    return jnp.where(keep, jnp.concatenate(out, 0), 0.0)


def step(
    sizes, e_hbm, h_hbm, ef_hbm, ec_hbm, hc_hbm, dft_hbm, modes_hbm,
    mask_hbm, omega_hbm, pidx_hbm, powner_hbm, mon_hbm,
    en, hn, dn, mon_out,
    ef, ec, hc, modes, mask_ref, omega_ref, pidx_ref, powner_ref, mon_ref,
    hx_in, hy_in, hz_in, ex_in, ey_in, ez_in, hy_out, ey_out, mine, rows,
    load_sems, h_send, h_recv, e_send, e_recv, all_send, all_recv, known_sems,
):
    n_gx, n_gy, n_gz = sizes
    n = n_gx * n_gy * n_gz
    a, b, c = lax.axis_index("gx"), lax.axis_index("gy"), lax.axis_index("gz")
    stride_x, stride_y = n_gy * n_gz, n_gz
    me = a * stride_x + b * stride_y + c
    nx, nz, ny = ec.shape
    zt = nz // 8

    lines = [(a, n_gx, stride_x), (b, n_gy, stride_y), (c, n_gz, 1)]
    partners = [
        [me + (lax.rem(at + k, size) - at) * stride for k in range(1, size)]
        for at, size, stride in lines
    ]

    barrier = pltpu.get_barrier_semaphore()
    loads = [
        pltpu.make_async_copy(src, dst, load_sems.at[i])
        for i, (src, dst) in enumerate(
            [(h_hbm, hn), (e_hbm, en), (ec_hbm, ec), (modes_hbm, modes), (hc_hbm, hc), (ef_hbm, ef), (dft_hbm, dn),
             (mask_hbm, mask_ref), (omega_hbm, omega_ref), (pidx_hbm, pidx_ref), (powner_hbm, powner_ref), (mon_hbm, mon_ref)]
        )
    ]
    for load in loads[:3]:
        load.start()
    for line in partners:
        for dev in line:
            pl.semaphore_signal(
                barrier, inc=1, device_id=dev, device_id_type=pl.DeviceIdType.LOGICAL
            )
    for load in loads[7:] + loads[3:7]:
        load.start()

    def remote(src, dst, send, recv, dev):
        return pltpu.make_async_remote_copy(
            src_ref=src, dst_ref=dst, send_sem=send, recv_sem=recv,
            device_id=dev, device_id_type=pl.DeviceIdType.LOGICAL,
        )

    up = [(a < n_gx - 1, stride_x), (b < n_gy - 1, stride_y), (c < n_gz - 1, 1)]
    down = [(a > 0, stride_x), (b > 0, stride_y), (c > 0, 1)]
    h_copies = [
        remote(src, dst, h_send.at[i], h_recv.at[i], jnp.where(up[i][0], me + up[i][1], 0))
        for i, (src, dst) in enumerate(
            [(hn.at[1:3, nx - 1], hx_in), (hy_out, hy_in), (hn.at[0:2, :, nz - 1], hz_in)]
        )
    ]
    e_copies = [
        remote(src, dst, e_send.at[i], e_recv.at[i], jnp.where(down[i][0], me - down[i][1], 0))
        for i, (src, dst) in enumerate(
            [(en.at[1:3, 0], ex_in), (ey_out, ey_in), (en.at[0:2, :, 0], ez_in)]
        )
    ]

    row = lax.broadcasted_iota(jnp.int32, (nz, ny), 0)
    lane = lax.broadcasted_iota(jnp.int32, (nz, ny), 1)
    lane8 = lax.broadcasted_iota(jnp.int32, (8, 128), 1)

    loads[0].wait()
    hy_out[...] = pack_lane(
        [hn[comp, x] for comp in (0, 2) for x in range(nx)], ny - 1, lane8
    )
    pl.semaphore_wait(barrier, sum(map(len, partners)))
    for i in (0, 2, 1):
        pl.when(up[i][0])(h_copies[i].start)

    def tell(line, sem):
        for dev in line:
            pl.semaphore_signal(
                sem, inc=1, device_id=dev, device_id_type=pl.DeviceIdType.LOGICAL
            )

    tell(partners[1], known_sems.at[0])

    for load in loads[7:]:
        load.wait()
    sub8 = lax.broadcasted_iota(jnp.int32, (8, 128), 0)
    angle_rows = jnp.zeros((8, 128), jnp.float32)
    angle_lanes = jnp.zeros((8, 128), jnp.float32)
    for f in range(NF):
        angle_rows = jnp.where(sub8 == f, omega_ref[f], angle_rows)
        angle_lanes = jnp.where((lane8 == f) | (lane8 == f + NF), omega_ref[f], angle_lanes)
    cosines, sines = jnp.cos(angle_rows), -jnp.sin(angle_rows)
    phase_lanes = jnp.where(lane8 < NF, jnp.cos(angle_lanes), -jnp.sin(angle_lanes))
    weight = jnp.zeros((8, 128), jnp.float32)
    for k in range(ny // BY):
        weight = jnp.where(lane8 // BY == k, mask_ref[0, 0, k].astype(jnp.float32), weight)
    weight = jnp.concatenate([weight] * zt, 0)

    loads[1].wait()
    loads[2].wait()

    def low(plane, axis):
        first = (row if axis == 0 else lane) == 0
        return plane - jnp.where(first, 0.0, pltpu.roll(plane, 1, axis))

    for x in range(nx):
        h0, h1, h2 = hn[0, x], hn[1, x], hn[2, x]
        d1 = h1 - hn[1, x - 1] if x else h1
        d2 = h2 - hn[2, x - 1] if x else h2
        coef = ec[x]
        en[0, x] = en[0, x] - coef * (low(h2, 1) - low(h1, 0))
        en[1, x] = en[1, x] - coef * (low(h0, 0) - d2)
        en[2, x] = en[2, x] - coef * (d1 - low(h0, 1))

    if n_gy > 1:
        pl.semaphore_wait(known_sems.at[0], n_gy - 1)
    tell(partners[2], known_sems.at[1])

    for i, landing in enumerate((hx_in, hy_in, hz_in)):
        pl.when(down[i][0])(h_copies[i].wait_recv)

        @pl.when(jnp.logical_not(down[i][0]))
        def _(landing=landing):
            landing[...] = jnp.zeros_like(landing)

    packed = hy_in[...]
    for x in range(nx):
        coef = ec[x]
        y0 = unpack_lane(packed, x * zt, zt, 0, lane == 0)
        y2 = unpack_lane(packed, (nx + x) * zt, zt, 0, lane == 0)
        z0 = jnp.where(sub8 == 0, hz_in[0, x : x + 1, :], 0.0)
        z1 = jnp.where(sub8 == 0, hz_in[1, x : x + 1, :], 0.0)
        rest = jnp.zeros((nz - 8, ny), jnp.float32)
        z0, z1 = jnp.concatenate([z0, rest], 0), jnp.concatenate([z1, rest], 0)
        add0, add1, add2 = y2 - z1, z0, -y0
        if x == 0:
            add1 = add1 - hx_in[1]
            add2 = add2 + hx_in[0]
        en[0, x] = en[0, x] + coef * add0
        en[1, x] = en[1, x] + coef * add1
        en[2, x] = en[2, x] + coef * add2

    loads[3].wait()
    share = jnp.zeros((8, 128), jnp.float32)
    for p in range(NP):
        x_of = pidx_ref[p] - a * nx
        inside = (x_of >= 0) & (x_of < nx)
        at = jnp.clip(x_of, 0, nx - 1)
        both = modes[p, 0] * en[1, at] + modes[p, 1] * en[2, at]
        total = functools.reduce(jnp.add, tiles(both))
        total = jnp.sum(jnp.sum(total, axis=0, keepdims=True), axis=1, keepdims=True)
        total = jnp.where(inside, total, 0.0)
        share = jnp.where(lane8 == p, total, share)

    mine[...] = share[0:1]
    if n_gz > 1:
        pl.semaphore_wait(known_sems.at[1], n_gz - 1)

    def send_row(k, _):
        remote(mine, rows.at[k - 1], all_send, all_recv, lax.rem(me + k, n)).start()
        return 0

    lax.fori_loop(1, n, send_row, 0, unroll=n <= UNROLL)
    for i in (0, 2):
        pl.when(down[i][0])(e_copies[i].start)
    ey_out[...] = pack_lane([en[comp, x] for comp in (0, 2) for x in range(nx)], 0, lane8)
    pl.when(down[1][0])(e_copies[1].start)

    for i in range(3):
        pl.when(up[i][0])(h_copies[i].wait_send)
    loads[4].wait()

    def high(plane, axis):
        last = (row == nz - 1) if axis == 0 else (lane == ny - 1)
        return jnp.where(last, 0.0, pltpu.roll(plane, plane.shape[axis] - 1, axis)) - plane

    for x in range(nx):
        e0, e1, e2 = en[0, x], en[1, x], en[2, x]
        d1 = en[1, x + 1] - e1 if x < nx - 1 else -e1
        d2 = en[2, x + 1] - e2 if x < nx - 1 else -e2
        coef = hc[x]
        hn[0, x] = hn[0, x] + coef * (high(e2, 1) - high(e1, 0))
        hn[1, x] = hn[1, x] + coef * (high(e0, 0) - d2)
        hn[2, x] = hn[2, x] + coef * (d1 - high(e0, 1))

    loads[5].wait()
    loads[6].wait()
    for x in range(nx):
        product = weight * (ef[0, x] * en[0, x] + ef[1, x] * en[1, x] + ef[2, x] * en[2, x])
        for f in range(NF):
            dn[f, x] = dn[f, x] + cosines[f : f + 1] * product
            dn[NF + f, x] = dn[NF + f, x] + sines[f : f + 1] * product

    for i, landing in enumerate((ex_in, ey_in, ez_in)):
        pl.when(up[i][0])(e_copies[i].wait_recv)

        @pl.when(jnp.logical_not(up[i][0]))
        def _(landing=landing):
            landing[...] = jnp.zeros_like(landing)

    packed = ey_in[...]
    for x in range(nx):
        coef = hc[x]
        y0 = unpack_lane(packed, x * zt, zt, ny - 1, lane == ny - 1)
        y2 = unpack_lane(packed, (nx + x) * zt, zt, ny - 1, lane == ny - 1)
        z0 = jnp.where(sub8 == 7, ez_in[0, x : x + 1, :], 0.0)
        z1 = jnp.where(sub8 == 7, ez_in[1, x : x + 1, :], 0.0)
        rest = jnp.zeros((nz - 8, ny), jnp.float32)
        z0, z1 = jnp.concatenate([rest, z0], 0), jnp.concatenate([rest, z1], 0)
        add0, add1, add2 = y2 - z1, z0, -y0
        if x == nx - 1:
            add1 = add1 - ex_in[1]
            add2 = add2 + ex_in[0]
        hn[0, x] = hn[0, x] + coef * add0
        hn[1, x] = hn[1, x] + coef * add1
        hn[2, x] = hn[2, x] + coef * add2
    for i in range(3):
        pl.when(down[i][0])(e_copies[i].wait_send)

    remote(rows, rows, all_send, all_recv, me).wait()
    intersection = jnp.sum(rows[...], axis=0) + mine[...]
    lane1 = lax.broadcasted_iota(jnp.int32, (1, 128), 1)
    owned = jnp.zeros((1, 128), jnp.float32)
    for p in range(NP):
        owned = jnp.where(lane1 == p, (powner_ref[p] == me).astype(jnp.float32), owned)
    total = jnp.sum(owned * intersection, axis=1, keepdims=True)
    mon_out[...] = mon_ref[...] + total * phase_lanes[0:1, : 2 * NF]


def write_out(en, hn, dn, mon, en_out, hn_out, dn_out, mon_out, sems):
    parts = 4
    size = dn.shape[0] // parts
    pairs = [(dn.at[pl.ds(i * size, size)], dn_out.at[pl.ds(i * size, size)]) for i in range(parts)]
    pairs += [(en, en_out), (hn, hn_out), (mon, mon_out)]
    copies = [pltpu.make_async_copy(src, dst, sems.at[i]) for i, (src, dst) in enumerate(pairs)]
    for copy in copies:
        copy.start()
    for copy in copies:
        copy.wait()


def body(sizes, e_field, h_field, e_forward, e_coeff, h_coeff, dft_acc, design_mask,
         omega_t, port_index, port_owner, port_modes, monitor_acc):
    nx, nz, ny = e_coeff.shape
    n = sizes[0] * sizes[1] * sizes[2]
    f32 = jnp.float32
    hbm = pl.BlockSpec(memory_space=pltpu.HBM)
    vmem = pl.BlockSpec(memory_space=pltpu.VMEM)
    far = lambda x: pltpu.with_memory_space_constraint(x, pltpu.HBM)
    held = pl.pallas_call(
        functools.partial(step, sizes),
        out_shape=[
            pltpu.VMEM(e_field.shape, f32),
            pltpu.VMEM(h_field.shape, f32),
            pltpu.VMEM(dft_acc.shape, f32),
            pltpu.VMEM(monitor_acc.shape, f32),
        ],
        in_specs=[hbm] * 12,
        out_specs=[vmem] * 4,
        scratch_shapes=[
            pltpu.VMEM(e_forward.shape, f32),
            pltpu.VMEM(e_coeff.shape, f32),
            pltpu.VMEM(h_coeff.shape, f32),
            pltpu.VMEM(port_modes.shape, f32),
            pltpu.SMEM(design_mask.shape, jnp.int32),
            pltpu.SMEM(omega_t.shape, f32),
            pltpu.SMEM(port_index.shape, jnp.int32),
            pltpu.SMEM(port_owner.shape, jnp.int32),
            pltpu.VMEM(monitor_acc.shape, f32),
            pltpu.VMEM((2, nz, ny), f32),
            pltpu.VMEM((8, 128), f32),
            pltpu.VMEM((2, nx, ny), f32),
            pltpu.VMEM((2, nz, ny), f32),
            pltpu.VMEM((8, 128), f32),
            pltpu.VMEM((2, nx, ny), f32),
            pltpu.VMEM((8, 128), f32),
            pltpu.VMEM((8, 128), f32),
            pltpu.VMEM((1, 128), f32),
            pltpu.VMEM((n - 1, 1, 128), f32),
            pltpu.SemaphoreType.DMA((12,)),
            pltpu.SemaphoreType.DMA((3,)),
            pltpu.SemaphoreType.DMA((3,)),
            pltpu.SemaphoreType.DMA((3,)),
            pltpu.SemaphoreType.DMA((3,)),
            pltpu.SemaphoreType.DMA,
            pltpu.SemaphoreType.DMA,
            pltpu.SemaphoreType.REGULAR((2,)),
        ],
        compiler_params=pltpu.CompilerParams(
            collective_id=0, has_side_effects=True, vmem_limit_bytes=24 * 2**20
        ),
        name="yee_step",
    )(*map(far, (e_field, h_field, e_forward, e_coeff, h_coeff, dft_acc, port_modes,
      design_mask, omega_t, port_index, port_owner, monitor_acc)))
    shape = lambda x: jax.ShapeDtypeStruct(x.shape, f32)
    return pl.pallas_call(
        write_out,
        out_shape=[shape(x) for x in (e_field, h_field, dft_acc, monitor_acc)],
        in_specs=[vmem] * 4,
        out_specs=[hbm] * 4,
        scratch_shapes=[pltpu.SemaphoreType.DMA((7,))],
        name="write_out",
    )(*[pltpu.with_memory_space_constraint(x, pltpu.VMEM) for x in held])


def solution(mesh):
    grid = P(None, "gx", "gz", "gy")
    brick = P("gx", "gz", "gy")
    own = P(("gx", "gy", "gz"), None)
    sizes = tuple(mesh.shape[axis] for axis in ("gx", "gy", "gz"))
    in_specs = (grid, grid, grid, brick, brick, grid, brick, P(), P(), P(),
                P(None, None, "gz", "gy"), own)
    return jax.shard_map(
        functools.partial(body, sizes), mesh=mesh, in_specs=in_specs,
        out_specs=(grid, grid, grid, own), check_vma=False,
    )
```

profile of v0, /device:TPU:0, one launch (start us, length us, event | category | flops | bytes accessed | tf_op | source)
XLA Modules:
  0.0 15.4 jit_solution(1090504879298068652)
XLA Ops:
  0.6 13.1 %yee_step.1 = (f32[3,8,32,128]{3,2,1,0:T(8,128)S(1)}, f32[3,8,32,128]{3,2,1,0:T(8,128)S(1)}, f32[16,8,32,128]{3,2,1,0:T(8,128)S(1)}, f32[1,16]{1,0:T(1,128)S(1)}) custom-call(f32[3,8,32,128]{3,2,1,0:T(8,128)} %e_hbm.1, f32[3,8,32,128]{3,2,1,0:T(8,128)} %h_hbm.1, f32[3,8,32,128]{3,2,1,0:T(8,128)} %ef_hbm.1, f32[8,32,128]{2,1,0:T(8,128)} %ec_hbm.1, ...), custom_call_target="tpu_custom_call" | custom-call | tf_op jit(solution)/shard_map/yee_step/pallas_call | solution.py:283
  13.7 1.6 %write_out.1 = (f32[3,8,32,128]{3,2,1,0:T(8,128)}, f32[3,8,32,128]{3,2,1,0:T(8,128)}, f32[16,8,32,128]{3,2,1,0:T(8,128)}, f32[1,16]{1,0:T(1,128)}) custom-call(f32[3,8,32,128]{3,2,1,0:T(8,128)S(1)} %get-tuple-element.8.en, f32[3,8,32,128]{3,2,1,0:T(8,128)S(1)} %get-tuple-element.9.hn, f32[16,8,32,128]{3,2,1,0:T(8,128)S(1)} %get-tuple-element.10.dn, ...), custom_call_target="tpu_custom_call" | custom-call | tf_op jit(solution)/shard_map/write_out/pallas_call | solution.py:329
where the time goes:
time: 15.5 us; the launch traced here: 15.4 us
  Pallas kernels  14.7 us (95%)
  between operations  0.64 us (4%)
    pallas_call x1, Pallas kernels, body(): pl.pallas_call(functools.partial(step, sizes), out_shape=[pltpu.VMEM(e_fi...  13.1 us
    pallas_call x1, Pallas kernels, body(): pl.pallas_call(write_out, out_shape=[shape(x) for x in (e_field, h_field,...  1.63 us

commit v1 on v0

--- a/solution.py
+++ b/solution.py
@@ -39,7 +39,8 @@
     en, hn, dn, mon_out,
     ef, ec, hc, modes, mask_ref, omega_ref, pidx_ref, powner_ref, mon_ref,
     hx_in, hy_in, hz_in, ex_in, ey_in, ez_in, hy_out, ey_out, mine, rows,
-    load_sems, h_send, h_recv, e_send, e_recv, all_send, all_recv, known_sems,
+    cx_in, cy_in, cz_in, cy_out, cz_out,
+    load_sems, h_send, h_recv, e_send, e_recv, c_send, c_recv, all_send, all_recv, known_sems,
 ):
     n_gx, n_gy, n_gz = sizes
     n = n_gx * n_gy * n_gz
@@ -63,15 +64,15 @@
              (mask_hbm, mask_ref), (omega_hbm, omega_ref), (pidx_hbm, pidx_ref), (powner_hbm, powner_ref), (mon_hbm, mon_ref)]
         )
     ]
-    for load in loads[:3]:
-        load.start()
+    for i in (9, 2, 3, 0, 1):
+        loads[i].start()
     for line in partners:
         for dev in line:
             pl.semaphore_signal(
                 barrier, inc=1, device_id=dev, device_id_type=pl.DeviceIdType.LOGICAL
             )
-    for load in loads[7:] + loads[3:7]:
-        load.start()
+    for i in (7, 8, 10, 11, 4, 5, 6):
+        loads[i].start()
 
     def remote(src, dst, send, recv, dev):
         return pltpu.make_async_remote_copy(
@@ -94,17 +95,16 @@
         )
     ]
 
+    c_copies = [
+        remote(src, dst, c_send.at[i], c_recv.at[i], jnp.where(down[i][0], me - down[i][1], 0))
+        for i, (src, dst) in enumerate([(ec.at[0], cx_in), (cy_out, cy_in), (cz_out, cz_in)])
+    ]
+
     row = lax.broadcasted_iota(jnp.int32, (nz, ny), 0)
     lane = lax.broadcasted_iota(jnp.int32, (nz, ny), 1)
     lane8 = lax.broadcasted_iota(jnp.int32, (8, 128), 1)
 
-    loads[0].wait()
-    hy_out[...] = pack_lane(
-        [hn[comp, x] for comp in (0, 2) for x in range(nx)], ny - 1, lane8
-    )
-    pl.semaphore_wait(barrier, sum(map(len, partners)))
-    for i in (0, 2, 1):
-        pl.when(up[i][0])(h_copies[i].start)
+    sub8 = lax.broadcasted_iota(jnp.int32, (8, 128), 0)
 
     def tell(line, sem):
         for dev in line:
@@ -112,11 +112,32 @@
                 sem, inc=1, device_id=dev, device_id_type=pl.DeviceIdType.LOGICAL
             )
 
+    for i in (9, 2, 3):
+        loads[i].wait()
+    ports = []
+    for p in range(NP):
+        x_of = pidx_ref[p] - a * nx
+        ports.append(((x_of >= 0) & (x_of < nx), x_of == nx, jnp.clip(x_of, 0, nx - 1)))
+    cy_out[...] = pack_lane(
+        [modes[p, 1] * ec[at] for p, (_, _, at) in enumerate(ports)], 0, lane8
+    )
+    for p, (_, _, at) in enumerate(ports):
+        cz_out[p : p + 1] = modes[p, 0, 0:1] * ec[at, 0:1]
+
+    pl.semaphore_wait(barrier, sum(map(len, partners)))
+    for i in (1, 0, 2):
+        pl.when(down[i][0])(c_copies[i].start)
     tell(partners[1], known_sems.at[0])
 
-    for load in loads[7:]:
-        load.wait()
-    sub8 = lax.broadcasted_iota(jnp.int32, (8, 128), 0)
+    loads[0].wait()
+    hy_out[...] = pack_lane(
+        [hn[comp, x] for comp in (0, 2) for x in range(nx)], ny - 1, lane8
+    )
+    for i in (0, 2, 1):
+        pl.when(up[i][0])(h_copies[i].start)
+
+    for i in (7, 8, 10, 11):
+        loads[i].wait()
     angle_rows = jnp.zeros((8, 128), jnp.float32)
     angle_lanes = jnp.zeros((8, 128), jnp.float32)
     for f in range(NF):
@@ -130,7 +151,6 @@
     weight = jnp.concatenate([weight] * zt, 0)
 
     loads[1].wait()
-    loads[2].wait()
 
     def low(plane, axis):
         first = (row if axis == 0 else lane) == 0
@@ -148,6 +168,37 @@
     if n_gy > 1:
         pl.semaphore_wait(known_sems.at[0], n_gy - 1)
     tell(partners[2], known_sems.at[1])
+
+    h_packed = pack_lane([hn[0, at] for _, _, at in ports], ny - 1, lane8)
+    partial = []
+    for p, (inside, _, at) in enumerate(ports):
+        both = modes[p, 0] * en[1, at] + modes[p, 1] * en[2, at]
+        partial.append(jnp.where(inside, functools.reduce(jnp.add, tiles(both)), 0.0))
+
+    for i, landing in enumerate((cx_in, cy_in, cz_in)):
+        pl.when(up[i][0])(c_copies[i].wait_recv)
+
+        @pl.when(jnp.logical_not(up[i][0]))
+        def _(landing=landing):
+            landing[...] = jnp.zeros_like(landing)
+
+    y_part = h_packed * cy_in[...]
+    for p, (inside, above, at) in enumerate(ports):
+        x_part = cx_in[...] * (modes[p, 1] * hn[1, nx - 1] - modes[p, 0] * hn[2, nx - 1])
+        x_part = jnp.where(above, functools.reduce(jnp.add, tiles(x_part)), 0.0)
+        yz_part = jnp.where(sub8 == 0, cz_in[p : p + 1] * hn[0, at, nz - 1 : nz], 0.0)
+        yz_part = yz_part - jnp.where(lane8 // zt == p, y_part, 0.0)
+        total = partial[p] + x_part + jnp.where(inside, yz_part, 0.0)
+        mine[p : p + 1] = jnp.sum(total, axis=0, keepdims=True)
+
+    if n_gz > 1:
+        pl.semaphore_wait(known_sems.at[1], n_gz - 1)
+
+    def send_row(k, _):
+        remote(mine, rows.at[k - 1], all_send, all_recv, lax.rem(me + k, n)).start()
+        return 0
+
+    lax.fori_loop(1, n, send_row, 0, unroll=n <= UNROLL)
 
     for i, landing in enumerate((hx_in, hy_in, hz_in)):
         pl.when(down[i][0])(h_copies[i].wait_recv)
@@ -173,27 +224,6 @@
         en[1, x] = en[1, x] + coef * add1
         en[2, x] = en[2, x] + coef * add2
 
-    loads[3].wait()
-    share = jnp.zeros((8, 128), jnp.float32)
-    for p in range(NP):
-        x_of = pidx_ref[p] - a * nx
-        inside = (x_of >= 0) & (x_of < nx)
-        at = jnp.clip(x_of, 0, nx - 1)
-        both = modes[p, 0] * en[1, at] + modes[p, 1] * en[2, at]
-        total = functools.reduce(jnp.add, tiles(both))
-        total = jnp.sum(jnp.sum(total, axis=0, keepdims=True), axis=1, keepdims=True)
-        total = jnp.where(inside, total, 0.0)
-        share = jnp.where(lane8 == p, total, share)
-
-    mine[...] = share[0:1]
-    if n_gz > 1:
-        pl.semaphore_wait(known_sems.at[1], n_gz - 1)
-
-    def send_row(k, _):
-        remote(mine, rows.at[k - 1], all_send, all_recv, lax.rem(me + k, n)).start()
-        return 0
-
-    lax.fori_loop(1, n, send_row, 0, unroll=n <= UNROLL)
     for i in (0, 2):
         pl.when(down[i][0])(e_copies[i].start)
     ey_out[...] = pack_lane([en[comp, x] for comp in (0, 2) for x in range(nx)], 0, lane8)
@@ -249,14 +279,16 @@
         hn[2, x] = hn[2, x] + coef * add2
     for i in range(3):
         pl.when(down[i][0])(e_copies[i].wait_send)
+        pl.when(down[i][0])(c_copies[i].wait_send)
 
     remote(rows, rows, all_send, all_recv, me).wait()
     intersection = jnp.sum(rows[...], axis=0) + mine[...]
-    lane1 = lax.broadcasted_iota(jnp.int32, (1, 128), 1)
-    owned = jnp.zeros((1, 128), jnp.float32)
+    port = lax.broadcasted_iota(jnp.int32, (NP, 128), 0)
+    owned = jnp.zeros((NP, 128), jnp.float32)
     for p in range(NP):
-        owned = jnp.where(lane1 == p, (powner_ref[p] == me).astype(jnp.float32), owned)
-    total = jnp.sum(owned * intersection, axis=1, keepdims=True)
+        owned = jnp.where(port == p, (powner_ref[p] == me).astype(jnp.float32), owned)
+    total = jnp.sum(owned * intersection, axis=0, keepdims=True)
+    total = jnp.sum(total, axis=1, keepdims=True)
     mon_out[...] = mon_ref[...] + total * phase_lanes[0:1, : 2 * NF]
 
 
@@ -308,9 +340,16 @@
             pltpu.VMEM((2, nx, ny), f32),
             pltpu.VMEM((8, 128), f32),
             pltpu.VMEM((8, 128), f32),
-            pltpu.VMEM((1, 128), f32),
-            pltpu.VMEM((n - 1, 1, 128), f32),
+            pltpu.VMEM((NP, 128), f32),
+            pltpu.VMEM((n - 1, NP, 128), f32),
+            pltpu.VMEM((nz, ny), f32),
+            pltpu.VMEM((8, 128), f32),
+            pltpu.VMEM((NP, 128), f32),
+            pltpu.VMEM((8, 128), f32),
+            pltpu.VMEM((NP, 128), f32),
             pltpu.SemaphoreType.DMA((12,)),
+            pltpu.SemaphoreType.DMA((3,)),
+            pltpu.SemaphoreType.DMA((3,)),
             pltpu.SemaphoreType.DMA((3,)),
             pltpu.SemaphoreType.DMA((3,)),
             pltpu.SemaphoreType.DMA((3,)),

time: 15.5 us -> 14.8 us (0.955)
  Pallas kernels: 14.7 us -> 14 us
    pallas_call x1, Pallas kernels: 13.1 us -> 12.4 us  [body(): pl.pallas_call(functools.partial(step, sizes), out_shape=[pltpu.VMEM(e_fi...]
where the time goes in v1:
time: 14.8 us; the launch traced here: 14.6 us
  Pallas kernels  14 us (95%)
  between operations  0.64 us (4%)
    pallas_call x1, Pallas kernels, body(): pl.pallas_call(functools.partial(step, sizes), out_shape=[pltpu.VMEM(e_fi...  12.4 us
    pallas_call x1, Pallas kernels, body(): pl.pallas_call(write_out, out_shape=[shape(x) for x in (e_field, h_field,...  1.63 us

profile of v1, /device:TPU:0, one launch (start us, length us, event | category | flops | bytes accessed | tf_op | source)
XLA Modules:
  0.0 14.6 jit_solution(17570163912513286125)
XLA Ops:
  0.6 12.4 %yee_step.1 = (f32[3,8,32,128]{3,2,1,0:T(8,128)S(1)}, f32[3,8,32,128]{3,2,1,0:T(8,128)S(1)}, f32[16,8,32,128]{3,2,1,0:T(8,128)S(1)}, f32[1,16]{1,0:T(1,128)S(1)}) custom-call(f32[3,8,32,128]{3,2,1,0:T(8,128)} %e_hbm.1, f32[3,8,32,128]{3,2,1,0:T(8,128)} %h_hbm.1, f32[3,8,32,128]{3,2,1,0:T(8,128)} %ef_hbm.1, f32[8,32,128]{2,1,0:T(8,128)} %ec_hbm.1, ...), custom_call_target="tpu_custom_call" | custom-call | tf_op jit(solution)/shard_map/yee_step/pallas_call | solution.py:315
  13.0 1.6 %write_out.1 = (f32[3,8,32,128]{3,2,1,0:T(8,128)}, f32[3,8,32,128]{3,2,1,0:T(8,128)}, f32[16,8,32,128]{3,2,1,0:T(8,128)}, f32[1,16]{1,0:T(1,128)}) custom-call(f32[3,8,32,128]{3,2,1,0:T(8,128)S(1)} %get-tuple-element.8.en, f32[3,8,32,128]{3,2,1,0:T(8,128)S(1)} %get-tuple-element.9.hn, f32[16,8,32,128]{3,2,1,0:T(8,128)S(1)} %get-tuple-element.10.dn, ...), custom_call_target="tpu_custom_call" | custom-call | tf_op jit(solution)/shard_map/write_out/pallas_call | solution.py:368

commit v2 on v1

--- a/solution.py
+++ b/solution.py
@@ -39,11 +39,12 @@
     en, hn, dn, mon_out,
     ef, ec, hc, modes, mask_ref, omega_ref, pidx_ref, powner_ref, mon_ref,
     hx_in, hy_in, hz_in, ex_in, ey_in, ez_in, hy_out, ey_out, mine, rows,
-    cx_in, cy_in, cz_in, cy_out, cz_out,
+    cx_in, cz_in, mz_in,
     load_sems, h_send, h_recv, e_send, e_recv, c_send, c_recv, all_send, all_recv, known_sems,
 ):
     n_gx, n_gy, n_gz = sizes
     n = n_gx * n_gy * n_gz
+    kinds = rows.shape[1]
     a, b, c = lax.axis_index("gx"), lax.axis_index("gy"), lax.axis_index("gz")
     stride_x, stride_y = n_gy * n_gz, n_gz
     me = a * stride_x + b * stride_y + c
@@ -96,13 +97,16 @@
     ]
 
     c_copies = [
-        remote(src, dst, c_send.at[i], c_recv.at[i], jnp.where(down[i][0], me - down[i][1], 0))
-        for i, (src, dst) in enumerate([(ec.at[0], cx_in), (cy_out, cy_in), (cz_out, cz_in)])
+        (i, remote(src, dst, c_send.at[k], c_recv.at[k], jnp.where(down[i][0], me - down[i][1], 0)))
+        for k, (i, src, dst) in enumerate(
+            [(0, ec_hbm.at[0], cx_in), (2, ec_hbm.at[:, 0], cz_in), (2, modes_hbm.at[:, 0, 0], mz_in)]
+        )
     ]
 
     row = lax.broadcasted_iota(jnp.int32, (nz, ny), 0)
     lane = lax.broadcasted_iota(jnp.int32, (nz, ny), 1)
     lane8 = lax.broadcasted_iota(jnp.int32, (8, 128), 1)
+    group = 128 // NP
 
     sub8 = lax.broadcasted_iota(jnp.int32, (8, 128), 0)
 
@@ -112,21 +116,9 @@
                 sem, inc=1, device_id=dev, device_id_type=pl.DeviceIdType.LOGICAL
             )
 
-    for i in (9, 2, 3):
-        loads[i].wait()
-    ports = []
-    for p in range(NP):
-        x_of = pidx_ref[p] - a * nx
-        ports.append(((x_of >= 0) & (x_of < nx), x_of == nx, jnp.clip(x_of, 0, nx - 1)))
-    cy_out[...] = pack_lane(
-        [modes[p, 1] * ec[at] for p, (_, _, at) in enumerate(ports)], 0, lane8
-    )
-    for p, (_, _, at) in enumerate(ports):
-        cz_out[p : p + 1] = modes[p, 0, 0:1] * ec[at, 0:1]
-
     pl.semaphore_wait(barrier, sum(map(len, partners)))
-    for i in (1, 0, 2):
-        pl.when(down[i][0])(c_copies[i].start)
+    for i, copy in c_copies:
+        pl.when(down[i][0])(copy.start)
     tell(partners[1], known_sems.at[0])
 
     loads[0].wait()
@@ -136,7 +128,7 @@
     for i in (0, 2, 1):
         pl.when(up[i][0])(h_copies[i].start)
 
-    for i in (7, 8, 10, 11):
+    for i in (7, 8, 9, 10, 11):
         loads[i].wait()
     angle_rows = jnp.zeros((8, 128), jnp.float32)
     angle_lanes = jnp.zeros((8, 128), jnp.float32)
@@ -150,7 +142,13 @@
         weight = jnp.where(lane8 // BY == k, mask_ref[0, 0, k].astype(jnp.float32), weight)
     weight = jnp.concatenate([weight] * zt, 0)
 
-    loads[1].wait()
+    for i in (1, 2, 3):
+        loads[i].wait()
+
+    ports = []
+    for p in range(NP):
+        x_of = pidx_ref[p] - a * nx
+        ports.append(((x_of >= 0) & (x_of < nx), x_of == nx, jnp.clip(x_of, 0, nx - 1)))
 
     def low(plane, axis):
         first = (row if axis == 0 else lane) == 0
@@ -169,36 +167,68 @@
         pl.semaphore_wait(known_sems.at[0], n_gy - 1)
     tell(partners[2], known_sems.at[1])
 
-    h_packed = pack_lane([hn[0, at] for _, _, at in ports], ny - 1, lane8)
     partial = []
     for p, (inside, _, at) in enumerate(ports):
         both = modes[p, 0] * en[1, at] + modes[p, 1] * en[2, at]
         partial.append(jnp.where(inside, functools.reduce(jnp.add, tiles(both)), 0.0))
 
-    for i, landing in enumerate((cx_in, cy_in, cz_in)):
-        pl.when(up[i][0])(c_copies[i].wait_recv)
+    def column(planes, lane_of):
+        packed = jnp.zeros((8, 128), jnp.float32)
+        for p, plane in enumerate(planes):
+            for q, tile in enumerate(tiles(plane)):
+                to = p * group + q
+                packed = jnp.where(lane8 == to, pltpu.roll(tile, (to - lane_of) % 128, 1), packed)
+        packed = pltpu.roll(packed, 0, 1, stride=zt, stride_axis=0)
+        return jnp.sum(packed, axis=0, keepdims=True)
+
+    columns = []
+    if n_gy > 1:
+        below = [jnp.where(inside, -hn[0, at], 0.0) for inside, _, at in ports]
+        above = [modes[p, 1] * ec[at] for p, (_, _, at) in enumerate(ports)]
+        if n_gy == 2:
+            edge = jnp.broadcast_to(b == 0, (nz, ny))
+            both = [jnp.where(edge, pltpu.roll(u, 1, 1), v) for u, v in zip(below, above)]
+            columns = [column(both, 0)]
+        else:
+            columns = [column(below, ny - 1), column(above, 0)]
+
+    x_parts = [
+        jnp.where(over, modes[p, 1] * hn[1, nx - 1] - modes[p, 0] * hn[2, nx - 1], 0.0)
+        for p, (_, over, _) in enumerate(ports)
+    ]
+    z_parts = [jnp.where(inside, hn[0, at, nz - 1 : nz], 0.0) for inside, _, at in ports]
+
+    for (i, copy), landing in zip(c_copies, (cx_in, cz_in, mz_in)):
+        pl.when(up[i][0])(copy.wait_recv)
 
         @pl.when(jnp.logical_not(up[i][0]))
         def _(landing=landing):
             landing[...] = jnp.zeros_like(landing)
 
-    y_part = h_packed * cy_in[...]
-    for p, (inside, above, at) in enumerate(ports):
-        x_part = cx_in[...] * (modes[p, 1] * hn[1, nx - 1] - modes[p, 0] * hn[2, nx - 1])
-        x_part = jnp.where(above, functools.reduce(jnp.add, tiles(x_part)), 0.0)
-        yz_part = jnp.where(sub8 == 0, cz_in[p : p + 1] * hn[0, at, nz - 1 : nz], 0.0)
-        yz_part = yz_part - jnp.where(lane8 // zt == p, y_part, 0.0)
-        total = partial[p] + x_part + jnp.where(inside, yz_part, 0.0)
-        mine[p : p + 1] = jnp.sum(total, axis=0, keepdims=True)
+    share = jnp.zeros((8, 128), jnp.float32)
+    for p, (_, _, at) in enumerate(ports):
+        x_part = functools.reduce(jnp.add, tiles(cx_in[...] * x_parts[p]))
+        z_part = mz_in[p : p + 1] * cz_in[pl.ds(at, 1)] * z_parts[p]
+        total = partial[p] + x_part + jnp.where(sub8 == 0, z_part, 0.0)
+        width = 128
+        while width > group:
+            width //= 2
+            total = total + pltpu.roll(total, width, 1)
+        share = jnp.where(lane8 // group == p, total, share)
+    mine[0, 0:1] = jnp.sum(share, axis=0, keepdims=True)
+    for k, vector in enumerate(columns):
+        mine[0, k + 1 : k + 2] = vector
+    rows[pl.ds(me, 1)] = mine[...]
 
     if n_gz > 1:
         pl.semaphore_wait(known_sems.at[1], n_gz - 1)
 
     def send_row(k, _):
-        remote(mine, rows.at[k - 1], all_send, all_recv, lax.rem(me + k, n)).start()
+        to = k + jnp.where(k >= me, 1, 0)
+        remote(mine.at[0], rows.at[me], all_send, all_recv, to).start()
         return 0
 
-    lax.fori_loop(1, n, send_row, 0, unroll=n <= UNROLL)
+    lax.fori_loop(0, n - 1, send_row, 0, unroll=n <= UNROLL)
 
     for i, landing in enumerate((hx_in, hy_in, hz_in)):
         pl.when(down[i][0])(h_copies[i].wait_recv)
@@ -223,9 +253,10 @@
         en[0, x] = en[0, x] + coef * add0
         en[1, x] = en[1, x] + coef * add1
         en[2, x] = en[2, x] + coef * add2
-
-    for i in (0, 2):
-        pl.when(down[i][0])(e_copies[i].start)
+        if x == 0:
+            pl.when(down[0][0])(e_copies[0].start)
+
+    pl.when(down[2][0])(e_copies[2].start)
     ey_out[...] = pack_lane([en[comp, x] for comp in (0, 2) for x in range(nx)], 0, lane8)
     pl.when(down[1][0])(e_copies[1].start)
 
@@ -279,16 +310,23 @@
         hn[2, x] = hn[2, x] + coef * add2
     for i in range(3):
         pl.when(down[i][0])(e_copies[i].wait_send)
-        pl.when(down[i][0])(c_copies[i].wait_send)
-
-    remote(rows, rows, all_send, all_recv, me).wait()
-    intersection = jnp.sum(rows[...], axis=0) + mine[...]
-    port = lax.broadcasted_iota(jnp.int32, (NP, 128), 0)
-    owned = jnp.zeros((NP, 128), jnp.float32)
+
+    for i, copy in c_copies:
+        pl.when(down[i][0])(copy.wait_send)
+
+    others = rows.at[pl.ds(0, n - 1)]
+    remote(others, others, all_send, all_recv, me).wait()
+    intersection = jnp.sum(rows[:, 0:1], axis=0)
+    if n_gy > 1:
+        grid = (n_gx, n_gy, n_gz, 1, 128)
+        lower = rows[:, 1:2].reshape(grid)[:, : n_gy - 1]
+        upper = rows[:, kinds - 1 : kinds].reshape(grid)[:, 1:]
+        intersection = intersection + jnp.sum(lower * upper, axis=(0, 1, 2))
+    port = lax.broadcasted_iota(jnp.int32, (1, 128), 1) // (128 // NP)
+    owned = jnp.zeros((1, 128), jnp.float32)
     for p in range(NP):
         owned = jnp.where(port == p, (powner_ref[p] == me).astype(jnp.float32), owned)
-    total = jnp.sum(owned * intersection, axis=0, keepdims=True)
-    total = jnp.sum(total, axis=1, keepdims=True)
+    total = jnp.sum(owned * intersection, axis=1, keepdims=True)
     mon_out[...] = mon_ref[...] + total * phase_lanes[0:1, : 2 * NF]
 
 
@@ -308,6 +346,7 @@
          omega_t, port_index, port_owner, port_modes, monitor_acc):
     nx, nz, ny = e_coeff.shape
     n = sizes[0] * sizes[1] * sizes[2]
+    kinds = min(sizes[1], 3)
     f32 = jnp.float32
     hbm = pl.BlockSpec(memory_space=pltpu.HBM)
     vmem = pl.BlockSpec(memory_space=pltpu.VMEM)
@@ -340,13 +379,11 @@
             pltpu.VMEM((2, nx, ny), f32),
             pltpu.VMEM((8, 128), f32),
             pltpu.VMEM((8, 128), f32),
-            pltpu.VMEM((NP, 128), f32),
-            pltpu.VMEM((n - 1, NP, 128), f32),
+            pltpu.VMEM((1, kinds, 128), f32),
+            pltpu.VMEM((n, kinds, 128), f32),
             pltpu.VMEM((nz, ny), f32),
-            pltpu.VMEM((8, 128), f32),
-            pltpu.VMEM((NP, 128), f32),
-            pltpu.VMEM((8, 128), f32),
-            pltpu.VMEM((NP, 128), f32),
+            pltpu.VMEM((nx, ny), f32),
+            pltpu.VMEM((NP, ny), f32),
             pltpu.SemaphoreType.DMA((12,)),
             pltpu.SemaphoreType.DMA((3,)),
             pltpu.SemaphoreType.DMA((3,)),

time: 14.8 us -> 14.6 us (0.986)
    pallas_call x1, Pallas kernels: 12.4 us -> 12.2 us  [body(): pl.pallas_call(functools.partial(step, sizes), out_shape=[pltpu.VMEM(e_fi...]
where the time goes in v2:
time: 14.6 us; the launch traced here: 14.5 us
  Pallas kernels  13.9 us (95%)
  between operations  0.64 us (4%)
    pallas_call x1, Pallas kernels, body(): pl.pallas_call(functools.partial(step, sizes), out_shape=[pltpu.VMEM(e_fi...  12.2 us
    pallas_call x1, Pallas kernels, body(): pl.pallas_call(write_out, out_shape=[shape(x) for x in (e_field, h_field,...  1.63 us

profile of v2, /device:TPU:0, one launch (start us, length us, event | category | flops | bytes accessed | tf_op | source)
XLA Modules:
  0.0 14.5 jit_solution(6439253173796899230)
XLA Ops:
  0.6 12.2 %yee_step.1 = (f32[3,8,32,128]{3,2,1,0:T(8,128)S(1)}, f32[3,8,32,128]{3,2,1,0:T(8,128)S(1)}, f32[16,8,32,128]{3,2,1,0:T(8,128)S(1)}, f32[1,16]{1,0:T(1,128)S(1)}) custom-call(f32[3,8,32,128]{3,2,1,0:T(8,128)} %e_hbm.1, f32[3,8,32,128]{3,2,1,0:T(8,128)} %h_hbm.1, f32[3,8,32,128]{3,2,1,0:T(8,128)} %ef_hbm.1, f32[8,32,128]{2,1,0:T(8,128)} %ec_hbm.1, ...), custom_call_target="tpu_custom_call" | custom-call | tf_op jit(solution)/shard_map/yee_step/pallas_call | solution.py:354
  12.9 1.6 %write_out.1 = (f32[3,8,32,128]{3,2,1,0:T(8,128)}, f32[3,8,32,128]{3,2,1,0:T(8,128)}, f32[16,8,32,128]{3,2,1,0:T(8,128)}, f32[1,16]{1,0:T(1,128)}) custom-call(f32[3,8,32,128]{3,2,1,0:T(8,128)S(1)} %get-tuple-element.8.en, f32[3,8,32,128]{3,2,1,0:T(8,128)S(1)} %get-tuple-element.9.hn, f32[16,8,32,128]{3,2,1,0:T(8,128)S(1)} %get-tuple-element.10.dn, ...), custom_call_target="tpu_custom_call" | custom-call | tf_op jit(solution)/shard_map/write_out/pallas_call | solution.py:405

commit v3 on v2

--- a/solution.py
+++ b/solution.py
@@ -36,11 +36,12 @@
 def step(
     sizes, e_hbm, h_hbm, ef_hbm, ec_hbm, hc_hbm, dft_hbm, modes_hbm,
     mask_hbm, omega_hbm, pidx_hbm, powner_hbm, mon_hbm,
-    en, hn, dn, mon_out,
+    en, hn, dn, rows, aux,
     ef, ec, hc, modes, mask_ref, omega_ref, pidx_ref, powner_ref, mon_ref,
-    hx_in, hy_in, hz_in, ex_in, ey_in, ez_in, hy_out, ey_out, mine, rows,
+    hx_in, hy_in, hz_in, ex_in, ey_in, ez_in, hy_out, ey_out, mine,
     cx_in, cz_in, mz_in,
-    load_sems, h_send, h_recv, e_send, e_recv, c_send, c_recv, all_send, all_recv, known_sems,
+    load_sems, h_send, h_recv, e_send, e_recv, c_send, c_recv, all_send, all_recv,
+    near_sems, far_sems, known_sems,
 ):
     n_gx, n_gy, n_gz = sizes
     n = n_gx * n_gy * n_gz
@@ -52,10 +53,22 @@
     zt = nz // 8
 
     lines = [(a, n_gx, stride_x), (b, n_gy, stride_y), (c, n_gz, 1)]
-    partners = [
-        [me + (lax.rem(at + k, size) - at) * stride for k in range(1, size)]
-        for at, size, stride in lines
-    ]
+
+    def signal(sem, dev):
+        pl.semaphore_signal(sem, inc=1, device_id=dev, device_id_type=pl.DeviceIdType.LOGICAL)
+
+    def tell(line, sem):
+        at, size, stride = line
+        for k in range(1, size):
+            signal(sem, me + (lax.rem(at + k, size) - at) * stride)
+
+    def far_upper(axis):
+        at, size, _ = lines[axis]
+        if size > 2:
+
+            @pl.when(at < size - 2)
+            def _():
+                pl.semaphore_wait(far_sems.at[axis], size - 2 - at)
 
     barrier = pltpu.get_barrier_semaphore()
     loads = [
@@ -65,15 +78,9 @@
              (mask_hbm, mask_ref), (omega_hbm, omega_ref), (pidx_hbm, pidx_ref), (powner_hbm, powner_ref), (mon_hbm, mon_ref)]
         )
     ]
-    for i in (9, 2, 3, 0, 1):
-        loads[i].start()
-    for line in partners:
-        for dev in line:
-            pl.semaphore_signal(
-                barrier, inc=1, device_id=dev, device_id_type=pl.DeviceIdType.LOGICAL
-            )
-    for i in (7, 8, 10, 11, 4, 5, 6):
-        loads[i].start()
+    for at, size, stride in lines:
+        for k in range(1, size):
+            pl.when(at + k < size)(functools.partial(signal, barrier, me + k * stride))
 
     def remote(src, dst, send, recv, dev):
         return pltpu.make_async_remote_copy(
@@ -110,23 +117,35 @@
 
     sub8 = lax.broadcasted_iota(jnp.int32, (8, 128), 0)
 
-    def tell(line, sem):
-        for dev in line:
-            pl.semaphore_signal(
-                sem, inc=1, device_id=dev, device_id_type=pl.DeviceIdType.LOGICAL
-            )
-
-    pl.semaphore_wait(barrier, sum(map(len, partners)))
+    @pl.when(me > 0)
+    def _():
+        pl.semaphore_wait(barrier, a + b + c)
+
     for i, copy in c_copies:
         pl.when(down[i][0])(copy.start)
-    tell(partners[1], known_sems.at[0])
+    for axis, (at, size, stride) in enumerate(lines):
+        for k in range(1, size if axis else 2):
+            sem = (far_sems if k > 1 else near_sems).at[axis]
+            pl.when(at >= k)(functools.partial(signal, sem, me - k * stride))
+
+    for i in (0, 9, 2, 1, 3):
+        loads[i].start()
+    for i in (7, 8, 10, 11, 4, 5, 6):
+        loads[i].start()
 
     loads[0].wait()
     hy_out[...] = pack_lane(
         [hn[comp, x] for comp in (0, 2) for x in range(nx)], ny - 1, lane8
     )
-    for i in (0, 2, 1):
-        pl.when(up[i][0])(h_copies[i].start)
+    for i in (2, 0, 1):
+
+        @pl.when(up[i][0])
+        def _(i=i):
+            pl.semaphore_wait(near_sems.at[i], 1)
+            h_copies[i].start()
+
+    far_upper(1)
+    tell(lines[1], known_sems.at[0])
 
     for i in (7, 8, 9, 10, 11):
         loads[i].wait()
@@ -141,6 +160,13 @@
     for k in range(ny // BY):
         weight = jnp.where(lane8 // BY == k, mask_ref[0, 0, k].astype(jnp.float32), weight)
     weight = jnp.concatenate([weight] * zt, 0)
+    port = lax.broadcasted_iota(jnp.int32, (1, 128), 1) // group
+    owned = jnp.zeros((1, 128), jnp.float32)
+    for p in range(NP):
+        owned = jnp.where(port == p, (powner_ref[p] == me).astype(jnp.float32), owned)
+    aux[0:1] = owned
+    aux[1:2] = phase_lanes[0:1]
+    aux[2:3, : 2 * NF] = mon_ref[...]
 
     for i in (1, 2, 3):
         loads[i].wait()
@@ -162,10 +188,6 @@
         en[0, x] = en[0, x] - coef * (low(h2, 1) - low(h1, 0))
         en[1, x] = en[1, x] - coef * (low(h0, 0) - d2)
         en[2, x] = en[2, x] - coef * (d1 - low(h0, 1))
-
-    if n_gy > 1:
-        pl.semaphore_wait(known_sems.at[0], n_gy - 1)
-    tell(partners[2], known_sems.at[1])
 
     partial = []
     for p, (inside, _, at) in enumerate(ports):
@@ -197,6 +219,11 @@
         for p, (_, over, _) in enumerate(ports)
     ]
     z_parts = [jnp.where(inside, hn[0, at, nz - 1 : nz], 0.0) for inside, _, at in ports]
+
+    if n_gy > 1:
+        pl.semaphore_wait(known_sems.at[0], n_gy - 1)
+    far_upper(2)
+    tell(lines[2], known_sems.at[1])
 
     for (i, copy), landing in zip(c_copies, (cx_in, cz_in, mz_in)):
         pl.when(up[i][0])(copy.wait_recv)
@@ -223,12 +250,19 @@
     if n_gz > 1:
         pl.semaphore_wait(known_sems.at[1], n_gz - 1)
 
-    def send_row(k, _):
-        to = k + jnp.where(k >= me, 1, 0)
-        remote(mine.at[0], rows.at[me], all_send, all_recv, to).start()
-        return 0
-
-    lax.fori_loop(0, n - 1, send_row, 0, unroll=n <= UNROLL)
+    for k in range(1, n_gx):
+        pl.when(a >= k)(functools.partial(signal, known_sems.at[2], me - k * stride_x))
+
+    def send_rows(plane):
+        def send_row(k, _):
+            to = plane * stride_x + k
+            pl.when(to != me)(remote(mine.at[0], rows.at[me], all_send, all_recv, to).start)
+            return 0
+
+        lax.fori_loop(0, stride_x, send_row, 0, unroll=n <= UNROLL)
+
+    for plane in range(n_gx):
+        pl.when(plane <= a)(functools.partial(send_rows, plane))
 
     for i, landing in enumerate((hx_in, hy_in, hz_in)):
         pl.when(down[i][0])(h_copies[i].wait_recv)
@@ -285,6 +319,13 @@
             dn[f, x] = dn[f, x] + cosines[f : f + 1] * product
             dn[NF + f, x] = dn[NF + f, x] + sines[f : f + 1] * product
 
+    @pl.when(a < n_gx - 1)
+    def _():
+        pl.semaphore_wait(known_sems.at[2], n_gx - 1 - a)
+
+    for plane in range(1, n_gx):
+        pl.when(plane > a)(functools.partial(send_rows, plane))
+
     for i, landing in enumerate((ex_in, ey_in, ez_in)):
         pl.when(up[i][0])(e_copies[i].wait_recv)
 
@@ -316,28 +357,27 @@
 
     others = rows.at[pl.ds(0, n - 1)]
     remote(others, others, all_send, all_recv, me).wait()
-    intersection = jnp.sum(rows[:, 0:1], axis=0)
-    if n_gy > 1:
-        grid = (n_gx, n_gy, n_gz, 1, 128)
-        lower = rows[:, 1:2].reshape(grid)[:, : n_gy - 1]
-        upper = rows[:, kinds - 1 : kinds].reshape(grid)[:, 1:]
-        intersection = intersection + jnp.sum(lower * upper, axis=(0, 1, 2))
-    port = lax.broadcasted_iota(jnp.int32, (1, 128), 1) // (128 // NP)
-    owned = jnp.zeros((1, 128), jnp.float32)
-    for p in range(NP):
-        owned = jnp.where(port == p, (powner_ref[p] == me).astype(jnp.float32), owned)
-    total = jnp.sum(owned * intersection, axis=1, keepdims=True)
-    mon_out[...] = mon_ref[...] + total * phase_lanes[0:1, : 2 * NF]
-
-
-def write_out(en, hn, dn, mon, en_out, hn_out, dn_out, mon_out, sems):
+
+
+def write_out(sizes, en, hn, dn, rows, aux, en_out, hn_out, dn_out, mon_out, mon, sems):
     parts = 4
     size = dn.shape[0] // parts
     pairs = [(dn.at[pl.ds(i * size, size)], dn_out.at[pl.ds(i * size, size)]) for i in range(parts)]
     pairs += [(en, en_out), (hn, hn_out), (mon, mon_out)]
     copies = [pltpu.make_async_copy(src, dst, sems.at[i]) for i, (src, dst) in enumerate(pairs)]
-    for copy in copies:
+    for copy in copies[:-1]:
         copy.start()
+    kinds = rows.shape[1]
+    n_gy = sizes[1]
+    intersection = jnp.sum(rows[:, 0:1], axis=0)
+    if n_gy > 1:
+        grid = (*sizes, 1, 128)
+        lower = rows[:, 1:2].reshape(grid)[:, : n_gy - 1]
+        upper = rows[:, kinds - 1 : kinds].reshape(grid)[:, 1:]
+        intersection = intersection + jnp.sum(lower * upper, axis=(0, 1, 2))
+    total = jnp.sum(aux[0:1] * intersection, axis=1, keepdims=True)
+    mon[...] = aux[2:3, : 2 * NF] + total * aux[1:2, : 2 * NF]
+    copies[-1].start()
     for copy in copies:
         copy.wait()
 
@@ -357,10 +397,11 @@
             pltpu.VMEM(e_field.shape, f32),
             pltpu.VMEM(h_field.shape, f32),
             pltpu.VMEM(dft_acc.shape, f32),
-            pltpu.VMEM(monitor_acc.shape, f32),
+            pltpu.VMEM((n, kinds, 128), f32),
+            pltpu.VMEM((3, 128), f32),
         ],
         in_specs=[hbm] * 12,
-        out_specs=[vmem] * 4,
+        out_specs=[vmem] * 5,
         scratch_shapes=[
             pltpu.VMEM(e_forward.shape, f32),
             pltpu.VMEM(e_coeff.shape, f32),
@@ -380,7 +421,6 @@
             pltpu.VMEM((8, 128), f32),
             pltpu.VMEM((8, 128), f32),
             pltpu.VMEM((1, kinds, 128), f32),
-            pltpu.VMEM((n, kinds, 128), f32),
             pltpu.VMEM((nz, ny), f32),
             pltpu.VMEM((nx, ny), f32),
             pltpu.VMEM((NP, ny), f32),
@@ -393,7 +433,9 @@
             pltpu.SemaphoreType.DMA((3,)),
             pltpu.SemaphoreType.DMA,
             pltpu.SemaphoreType.DMA,
-            pltpu.SemaphoreType.REGULAR((2,)),
+            pltpu.SemaphoreType.REGULAR((3,)),
+            pltpu.SemaphoreType.REGULAR((3,)),
+            pltpu.SemaphoreType.REGULAR((3,)),
         ],
         compiler_params=pltpu.CompilerParams(
             collective_id=0, has_side_effects=True, vmem_limit_bytes=24 * 2**20
@@ -403,11 +445,11 @@
       design_mask, omega_t, port_index, port_owner, monitor_acc)))
     shape = lambda x: jax.ShapeDtypeStruct(x.shape, f32)
     return pl.pallas_call(
-        write_out,
+        functools.partial(write_out, sizes),
         out_shape=[shape(x) for x in (e_field, h_field, dft_acc, monitor_acc)],
-        in_specs=[vmem] * 4,
+        in_specs=[vmem] * 5,
         out_specs=[hbm] * 4,
-        scratch_shapes=[pltpu.SemaphoreType.DMA((7,))],
+        scratch_shapes=[pltpu.VMEM(monitor_acc.shape, f32), pltpu.SemaphoreType.DMA((7,))],
         name="write_out",
     )(*[pltpu.with_memory_space_constraint(x, pltpu.VMEM) for x in held])
 

time: 14.6 us -> 14.5 us (level)
  Pallas kernels: 13.9 us -> 13.7 us
where the time goes in v3:
time: 14.5 us; the launch traced here: 14.4 us
  Pallas kernels  13.7 us (94%)
  between operations  0.64 us (4%)
    pallas_call x1, Pallas kernels, body(): pl.pallas_call(functools.partial(step, sizes), out_shape=[pltpu.VMEM(e_fi...  12.1 us
    pallas_call x1, Pallas kernels, body(): pl.pallas_call(functools.partial(write_out, sizes), out_shape=[shape(x) f...  1.63 us

profile of v3, /device:TPU:0, one launch (start us, length us, event | category | flops | bytes accessed | tf_op | source)
XLA Modules:
  0.0 14.4 jit_solution(8959661484789797511)
XLA Ops:
  0.6 12.1 %yee_step.1 = (f32[3,8,32,128]{3,2,1,0:T(8,128)S(1)}, f32[3,8,32,128]{3,2,1,0:T(8,128)S(1)}, f32[16,8,32,128]{3,2,1,0:T(8,128)S(1)}, f32[32,2,128]{2,1,0:T(2,128)S(1)}, f32[3,128]{1,0:T(4,128)S(1)}) custom-call(f32[3,8,32,128]{3,2,1,0:T(8,128)} %e_hbm.1, f32[3,8,32,128]{3,2,1,0:T(8,128)} %h_hbm.1, f32[3,8,32,128]{3,2,1,0:T(8,128)} %ef_hbm.1, ...), custom_call_target="tpu_custom_call" | custom-call | tf_op jit(solution)/shard_map/yee_step/pallas_call | solution.py:394
  12.7 1.6 %write_out.1 = (f32[3,8,32,128]{3,2,1,0:T(8,128)}, f32[3,8,32,128]{3,2,1,0:T(8,128)}, f32[16,8,32,128]{3,2,1,0:T(8,128)}, f32[1,16]{1,0:T(1,128)}) custom-call(f32[3,8,32,128]{3,2,1,0:T(8,128)S(1)} %get-tuple-element.9.en, f32[3,8,32,128]{3,2,1,0:T(8,128)S(1)} %get-tuple-element.10.hn, f32[16,8,32,128]{3,2,1,0:T(8,128)S(1)} %get-tuple-element.11.dn, ...), custom_call_target="tpu_custom_call" | custom-call | tf_op jit(solution)/shard_map/write_out/pallas_call | solution.py:447

commit v4 on v3

--- a/solution.py
+++ b/solution.py
@@ -39,7 +39,7 @@
     en, hn, dn, rows, aux,
     ef, ec, hc, modes, mask_ref, omega_ref, pidx_ref, powner_ref, mon_ref,
     hx_in, hy_in, hz_in, ex_in, ey_in, ez_in, hy_out, ey_out, mine,
-    cx_in, cz_in, mz_in,
+    cx_in, cz_in, mz_in, cx_out,
     load_sems, h_send, h_recv, e_send, e_recv, c_send, c_recv, all_send, all_recv,
     near_sems, far_sems, known_sems,
 ):
@@ -62,6 +62,11 @@
         for k in range(1, size):
             signal(sem, me + (lax.rem(at + k, size) - at) * stride)
 
+    def tell_line():
+        for k in range(1, n_gz):
+            pl.when(c + k < n_gz)(functools.partial(signal, known_sems.at[1], me + k))
+            pl.when(c >= k)(functools.partial(signal, known_sems.at[3], me - k))
+
     def far_upper(axis):
         at, size, _ = lines[axis]
         if size > 2:
@@ -78,6 +83,8 @@
              (mask_hbm, mask_ref), (omega_hbm, omega_ref), (pidx_hbm, pidx_ref), (powner_hbm, powner_ref), (mon_hbm, mon_ref)]
         )
     ]
+    first = pltpu.make_async_copy(ec_hbm.at[0], cx_out, load_sems.at[12])
+    first.start()
     for at, size, stride in lines:
         for k in range(1, size):
             pl.when(at + k < size)(functools.partial(signal, barrier, me + k * stride))
@@ -106,7 +113,7 @@
     c_copies = [
         (i, remote(src, dst, c_send.at[k], c_recv.at[k], jnp.where(down[i][0], me - down[i][1], 0)))
         for k, (i, src, dst) in enumerate(
-            [(0, ec_hbm.at[0], cx_in), (2, ec_hbm.at[:, 0], cz_in), (2, modes_hbm.at[:, 0, 0], mz_in)]
+            [(0, cx_out, cx_in), (2, ec_hbm.at[:, 0], cz_in), (2, modes_hbm.at[:, 0, 0], mz_in)]
         )
     ]
 
@@ -121,12 +128,14 @@
     def _():
         pl.semaphore_wait(barrier, a + b + c)
 
-    for i, copy in c_copies:
+    for i, copy in c_copies[1:]:
         pl.when(down[i][0])(copy.start)
     for axis, (at, size, stride) in enumerate(lines):
         for k in range(1, size if axis else 2):
             sem = (far_sems if k > 1 else near_sems).at[axis]
             pl.when(at >= k)(functools.partial(signal, sem, me - k * stride))
+    first.wait()
+    pl.when(down[0][0])(c_copies[0][1].start)
 
     for i in (0, 9, 2, 1, 3):
         loads[i].start()
@@ -223,7 +232,7 @@
     if n_gy > 1:
         pl.semaphore_wait(known_sems.at[0], n_gy - 1)
     far_upper(2)
-    tell(lines[2], known_sems.at[1])
+    tell_line()
 
     for (i, copy), landing in zip(c_copies, (cx_in, cz_in, mz_in)):
         pl.when(up[i][0])(copy.wait_recv)
@@ -247,22 +256,32 @@
         mine[0, k + 1 : k + 2] = vector
     rows[pl.ds(me, 1)] = mine[...]
 
-    if n_gz > 1:
-        pl.semaphore_wait(known_sems.at[1], n_gz - 1)
+    @pl.when(c > 0)
+    def _():
+        pl.semaphore_wait(known_sems.at[1], c)
+
+    def send_rows(plane, part):
+        def send_row(k, _):
+            to = plane * stride_x + k
+            near = k % n_gz <= c
+            wanted = {"near": near, "far": jnp.logical_not(near), "all": True}[part]
+            pl.when((to != me) & wanted)(remote(mine.at[0], rows.at[me], all_send, all_recv, to).start)
+            return 0
+
+        lax.fori_loop(0, stride_x, send_row, 0, unroll=n <= UNROLL)
+
+    for plane in range(n_gx):
+        pl.when(plane <= a)(functools.partial(send_rows, plane, "near"))
+
+    @pl.when(c < n_gz - 1)
+    def _():
+        pl.semaphore_wait(known_sems.at[3], n_gz - 1 - c)
+
+    for plane in range(n_gx):
+        pl.when(plane <= a)(functools.partial(send_rows, plane, "far"))
 
     for k in range(1, n_gx):
         pl.when(a >= k)(functools.partial(signal, known_sems.at[2], me - k * stride_x))
-
-    def send_rows(plane):
-        def send_row(k, _):
-            to = plane * stride_x + k
-            pl.when(to != me)(remote(mine.at[0], rows.at[me], all_send, all_recv, to).start)
-            return 0
-
-        lax.fori_loop(0, stride_x, send_row, 0, unroll=n <= UNROLL)
-
-    for plane in range(n_gx):
-        pl.when(plane <= a)(functools.partial(send_rows, plane))
 
     for i, landing in enumerate((hx_in, hy_in, hz_in)):
         pl.when(down[i][0])(h_copies[i].wait_recv)
@@ -324,7 +343,7 @@
         pl.semaphore_wait(known_sems.at[2], n_gx - 1 - a)
 
     for plane in range(1, n_gx):
-        pl.when(plane > a)(functools.partial(send_rows, plane))
+        pl.when(plane > a)(functools.partial(send_rows, plane, "all"))
 
     for i, landing in enumerate((ex_in, ey_in, ez_in)):
         pl.when(up[i][0])(e_copies[i].wait_recv)
@@ -424,7 +443,8 @@
             pltpu.VMEM((nz, ny), f32),
             pltpu.VMEM((nx, ny), f32),
             pltpu.VMEM((NP, ny), f32),
-            pltpu.SemaphoreType.DMA((12,)),
+            pltpu.VMEM((nz, ny), f32),
+            pltpu.SemaphoreType.DMA((13,)),
             pltpu.SemaphoreType.DMA((3,)),
             pltpu.SemaphoreType.DMA((3,)),
             pltpu.SemaphoreType.DMA((3,)),
@@ -435,7 +455,7 @@
             pltpu.SemaphoreType.DMA,
             pltpu.SemaphoreType.REGULAR((3,)),
             pltpu.SemaphoreType.REGULAR((3,)),
-            pltpu.SemaphoreType.REGULAR((3,)),
+            pltpu.SemaphoreType.REGULAR((4,)),
         ],
         compiler_params=pltpu.CompilerParams(
             collective_id=0, has_side_effects=True, vmem_limit_bytes=24 * 2**20

time: 14.5 us -> 14.5 us (level)
  no operation moved by 1% of the time
where the time goes in v4:
time: 14.5 us; the launch traced here: 14.3 us
  Pallas kernels  13.7 us (94%)
  between operations  0.64 us (4%)
    pallas_call x1, Pallas kernels, body(): pl.pallas_call(functools.partial(step, sizes), out_shape=[pltpu.VMEM(e_fi...  12 us
    pallas_call x1, Pallas kernels, body(): pl.pallas_call(functools.partial(write_out, sizes), out_shape=[shape(x) f...  1.63 us

profile of v4, /device:TPU:0, one launch (start us, length us, event | category | flops | bytes accessed | tf_op | source)
XLA Modules:
  0.0 14.3 jit_solution(2463265140536259662)
XLA Ops:
  0.6 12.0 %yee_step.1 = (f32[3,8,32,128]{3,2,1,0:T(8,128)S(1)}, f32[3,8,32,128]{3,2,1,0:T(8,128)S(1)}, f32[16,8,32,128]{3,2,1,0:T(8,128)S(1)}, f32[32,2,128]{2,1,0:T(2,128)S(1)}, f32[3,128]{1,0:T(4,128)S(1)}) custom-call(f32[3,8,32,128]{3,2,1,0:T(8,128)} %e_hbm.1, f32[3,8,32,128]{3,2,1,0:T(8,128)} %h_hbm.1, f32[3,8,32,128]{3,2,1,0:T(8,128)} %ef_hbm.1, ...), custom_call_target="tpu_custom_call" | custom-call | tf_op jit(solution)/shard_map/yee_step/pallas_call | solution.py:413
  12.7 1.6 %write_out.1 = (f32[3,8,32,128]{3,2,1,0:T(8,128)}, f32[3,8,32,128]{3,2,1,0:T(8,128)}, f32[16,8,32,128]{3,2,1,0:T(8,128)}, f32[1,16]{1,0:T(1,128)}) custom-call(f32[3,8,32,128]{3,2,1,0:T(8,128)S(1)} %get-tuple-element.9.en, f32[3,8,32,128]{3,2,1,0:T(8,128)S(1)} %get-tuple-element.10.hn, f32[16,8,32,128]{3,2,1,0:T(8,128)S(1)} %get-tuple-element.11.dn, ...), custom_call_target="tpu_custom_call" | custom-call | tf_op jit(solution)/shard_map/write_out/pallas_call | solution.py:467

commit v5 on v4

--- a/solution.py
+++ b/solution.py
@@ -277,11 +277,11 @@
     def _():
         pl.semaphore_wait(known_sems.at[3], n_gz - 1 - c)
 
+    for k in range(1, n_gx):
+        pl.when(a >= k)(functools.partial(signal, known_sems.at[2], me - k * stride_x))
+
     for plane in range(n_gx):
         pl.when(plane <= a)(functools.partial(send_rows, plane, "far"))
-
-    for k in range(1, n_gx):
-        pl.when(a >= k)(functools.partial(signal, known_sems.at[2], me - k * stride_x))
 
     for i, landing in enumerate((hx_in, hy_in, hz_in)):
         pl.when(down[i][0])(h_copies[i].wait_recv)
@@ -342,7 +342,7 @@
     def _():
         pl.semaphore_wait(known_sems.at[2], n_gx - 1 - a)
 
-    for plane in range(1, n_gx):
+    for plane in range(n_gx - 1, 0, -1):
         pl.when(plane > a)(functools.partial(send_rows, plane, "all"))
 
     for i, landing in enumerate((ex_in, ey_in, ez_in)):

time: 14.5 us -> 14.5 us (level)
  no operation moved by 1% of the time
where the time goes in v5:
time: 14.5 us; the launch traced here: 14.3 us
  Pallas kernels  13.7 us (94%)
  between operations  0.64 us (4%)
    pallas_call x1, Pallas kernels, body(): pl.pallas_call(functools.partial(step, sizes), out_shape=[pltpu.VMEM(e_fi...  12 us
    pallas_call x1, Pallas kernels, body(): pl.pallas_call(functools.partial(write_out, sizes), out_shape=[shape(x) f...  1.63 us

profile of v5, /device:TPU:0, one launch (start us, length us, event | category | flops | bytes accessed | tf_op | source)
XLA Modules:
  0.0 14.3 jit_solution(15556800626742096077)
XLA Ops:
  0.6 12.0 %yee_step.1 = (f32[3,8,32,128]{3,2,1,0:T(8,128)S(1)}, f32[3,8,32,128]{3,2,1,0:T(8,128)S(1)}, f32[16,8,32,128]{3,2,1,0:T(8,128)S(1)}, f32[32,2,128]{2,1,0:T(2,128)S(1)}, f32[3,128]{1,0:T(4,128)S(1)}) custom-call(f32[3,8,32,128]{3,2,1,0:T(8,128)} %e_hbm.1, f32[3,8,32,128]{3,2,1,0:T(8,128)} %h_hbm.1, f32[3,8,32,128]{3,2,1,0:T(8,128)} %ef_hbm.1, ...), custom_call_target="tpu_custom_call" | custom-call | tf_op jit(solution)/shard_map/yee_step/pallas_call | solution.py:413
  12.7 1.6 %write_out.1 = (f32[3,8,32,128]{3,2,1,0:T(8,128)}, f32[3,8,32,128]{3,2,1,0:T(8,128)}, f32[16,8,32,128]{3,2,1,0:T(8,128)}, f32[1,16]{1,0:T(1,128)}) custom-call(f32[3,8,32,128]{3,2,1,0:T(8,128)S(1)} %get-tuple-element.9.en, f32[3,8,32,128]{3,2,1,0:T(8,128)S(1)} %get-tuple-element.10.hn, f32[16,8,32,128]{3,2,1,0:T(8,128)S(1)} %get-tuple-element.11.dn, ...), custom_call_target="tpu_custom_call" | custom-call | tf_op jit(solution)/shard_map/write_out/pallas_call | solution.py:467

commit v6 on v5

--- a/solution.py
+++ b/solution.py
@@ -330,6 +330,13 @@
         hn[1, x] = hn[1, x] + coef * (high(e0, 0) - d2)
         hn[2, x] = hn[2, x] + coef * (d1 - high(e0, 1))
 
+    @pl.when(a < n_gx - 1)
+    def _():
+        pl.semaphore_wait(known_sems.at[2], n_gx - 1 - a)
+
+    for plane in range(n_gx - 1, 0, -1):
+        pl.when(plane > a)(functools.partial(send_rows, plane, "all"))
+
     loads[5].wait()
     loads[6].wait()
     for x in range(nx):
@@ -337,13 +344,6 @@
         for f in range(NF):
             dn[f, x] = dn[f, x] + cosines[f : f + 1] * product
             dn[NF + f, x] = dn[NF + f, x] + sines[f : f + 1] * product
-
-    @pl.when(a < n_gx - 1)
-    def _():
-        pl.semaphore_wait(known_sems.at[2], n_gx - 1 - a)
-
-    for plane in range(n_gx - 1, 0, -1):
-        pl.when(plane > a)(functools.partial(send_rows, plane, "all"))
 
     for i, landing in enumerate((ex_in, ey_in, ez_in)):
         pl.when(up[i][0])(e_copies[i].wait_recv)

time: 14.5 us -> 14.5 us (level)
  no operation moved by 1% of the time
where the time goes in v6:
time: 14.5 us; the launch traced here: 14.3 us
  Pallas kernels  13.7 us (94%)
  between operations  0.64 us (4%)
    pallas_call x1, Pallas kernels, body(): pl.pallas_call(functools.partial(step, sizes), out_shape=[pltpu.VMEM(e_fi...  12 us
    pallas_call x1, Pallas kernels, body(): pl.pallas_call(functools.partial(write_out, sizes), out_shape=[shape(x) f...  1.63 us

profile of v6, /device:TPU:0, one launch (start us, length us, event | category | flops | bytes accessed | tf_op | source)
XLA Modules:
  0.0 14.3 jit_solution(11239719873466509822)
XLA Ops:
  0.6 12.0 %yee_step.1 = (f32[3,8,32,128]{3,2,1,0:T(8,128)S(1)}, f32[3,8,32,128]{3,2,1,0:T(8,128)S(1)}, f32[16,8,32,128]{3,2,1,0:T(8,128)S(1)}, f32[32,2,128]{2,1,0:T(2,128)S(1)}, f32[3,128]{1,0:T(4,128)S(1)}) custom-call(f32[3,8,32,128]{3,2,1,0:T(8,128)} %e_hbm.1, f32[3,8,32,128]{3,2,1,0:T(8,128)} %h_hbm.1, f32[3,8,32,128]{3,2,1,0:T(8,128)} %ef_hbm.1, ...), custom_call_target="tpu_custom_call" | custom-call | tf_op jit(solution)/shard_map/yee_step/pallas_call | solution.py:413
  12.7 1.6 %write_out.1 = (f32[3,8,32,128]{3,2,1,0:T(8,128)}, f32[3,8,32,128]{3,2,1,0:T(8,128)}, f32[16,8,32,128]{3,2,1,0:T(8,128)}, f32[1,16]{1,0:T(1,128)}) custom-call(f32[3,8,32,128]{3,2,1,0:T(8,128)S(1)} %get-tuple-element.9.en, f32[3,8,32,128]{3,2,1,0:T(8,128)S(1)} %get-tuple-element.10.hn, f32[16,8,32,128]{3,2,1,0:T(8,128)S(1)} %get-tuple-element.11.dn, ...), custom_call_target="tpu_custom_call" | custom-call | tf_op jit(solution)/shard_map/write_out/pallas_call | solution.py:467
